TPU v7x, 128 devices: a whole 4x4x4 slice. The times are simulated.
128 devices in a mesh: row: 16 (over y_hi, x, core), col: 8 (over z, y_lo).
Axes of the slice: x: 4, y: 4 (y_hi: 2, y_lo: 2; y = y_hi * 2 + y_lo), z: 4, core: 2. Of those that a mesh axis runs over, the one named last changes fastest.
Arguments:
- cycle_inter: float32 [1536, 1536, 128], P(None, ('row', 'col')), may hold values from -6 to 6
- integrals: float32 [1536, 1536, 128], P(None, ('row', 'col')), may hold values from -0.005859375 to 0.005859375
Outputs:
- ladder: float32 [128, 128], P('row')
All inputs are finite; a program needn't handle non-finite values.
Results may differ from a plain program's by a relative error of at most 0.0003.
Values sent between devices are 32-bit elements; how exact they have to be, the bound alone decides.
No kernel may reach another device: no remote copies, remote signals or barrier semaphores. Data moves between devices by JAX's collectives and lax.ppermute only.
A program may use at most 128 MiB of HBM per device.

v0:
```python
import jax
import jax.numpy as jnp
from jax import lax
from jax.sharding import PartitionSpec as P


def body(cycle_inter, integrals):
    row_count = lax.axis_size("row")
    col_count = lax.axis_size("col")
    local_width = cycle_inter.shape[1]
    occupied = cycle_inter.shape[2]
    slab_pairs = integrals.shape[2]
    received = lax.all_to_all(cycle_inter, ("row", "col"), split_axis=0, concat_axis=1, tiled=True)
    amplitudes = cycle_inter - jnp.swapaxes(received, 0, 1)
    device_rank = lax.axis_index("row") * col_count + lax.axis_index("col")
    first_column = device_rank * local_width
    column_ids = first_column + jnp.arange(local_width, dtype=jnp.int32)
    block_rows = 128
    needed_blocks = (first_column + local_width + block_rows - 1) // block_rows

    def accumulate(block_index, summed):
        offset = block_index * block_rows
        amp_block = lax.dynamic_slice_in_dim(amplitudes, offset, block_rows, 0)
        integral_block = lax.dynamic_slice_in_dim(integrals, offset, block_rows, 0)
        row_ids = offset + jnp.arange(block_rows, dtype=jnp.int32)
        upper_mask = (row_ids[:, None] < column_ids[None, :]).astype(jnp.float32)
        amp_block = amp_block * upper_mask[:, :, None]
        return summed + jnp.einsum(
            "cdi,cda->ia", amp_block, integral_block, precision=lax.Precision.HIGHEST
        )

    partial_sum = lax.fori_loop(
        0, needed_blocks, accumulate, jnp.zeros((occupied, slab_pairs), jnp.float32)
    )
    owned_rows = occupied // row_count
    summed = lax.psum(partial_sum, ("row", "col"))
    return lax.dynamic_slice_in_dim(summed, lax.axis_index("row") * owned_rows, owned_rows, 0)


def solution(mesh):
    return jax.shard_map(
        body,
        mesh=mesh,
        in_specs=(P(None, ("row", "col"), None), P(None, ("row", "col"), None)),
        out_specs=P("row", None),
        check_vma=False,
    )
```

profile of v0, /device:TPU:1, one launch (start us, length us, event | category | flops | bytes accessed | tf_op | source)
XLA Modules:
  0.0 412.1 jit_solution(1875631772332710024)
XLA Ops:
  6.5 12.7 %copy.7 = f32[1536,12,128]{2,1,0:T(8,128)} copy(f32[1536,12,128]{2,0,1:T(8,128)} %param.4) | data formatting | bytes 18874368 | tf_op args[0]
  19.2 11.9 %all-to-all-start = ((f32[1536,12,128]{2,1,0:T(8,128)}), f32[1536,12,128]{2,1,0:T(8,128)}, u32[]{:S(2)}, u32[]{:S(2)}) async-start(f32[1536,12,128]{2,1,0:T(8,128)} %copy.7), calls=%async_computation | async-start | bytes 25165824 | tf_op jit(solution)/shard_map/all_to_all | solution.py:13
  31.1 0.0 all-reduce.2.cloned.1.call-start
  31.2 165.2 %all-to-all-done = f32[1536,12,128]{2,1,0:T(8,128)} async-done(((f32[1536,12,128]{2,1,0:T(8,128)}), f32[1536,12,128]{2,1,0:T(8,128)}, u32[]{:S(2)}, u32[]{:S(2)}) %all-to-all-start) | async-done | bytes 9437216 | tf_op jit(solution)/shard_map/all_to_all | solution.py:13
  196.3 10.3 %copy.9 = f32[12,128,12,128]{3,2,1,0:T(8,128)} copy(f32[12,128,12,128]{3,2,0,1:T(8,128)} %bitcast.2) | data formatting | bytes 18874368 | tf_op jit(solution)/shard_map/all_to_all | solution.py:13
  206.7 12.0 %all_to_all.16 = f32[12,1536,128]{2,1,0:T(8,128)} reshape(f32[12,128,12,128]{3,2,1,0:T(8,128)} %copy.9) | data formatting | bytes 18874368 | tf_op jit(solution)/shard_map/all_to_all | solution.py:13
  218.7 10.9 %bitcast_subtract_fusion = f32[1536,12,128]{2,0,1:T(8,128)} fusion(f32[1536,12,128]{2,0,1:T(8,128)} %param.4, f32[12,1536,128]{2,1,0:T(8,128)} %all_to_all.16), kind=kLoop, calls=%fused_computation.11 | loop fusion | flops 2359296 | bytes 28311552 | tf_op jit(solution)/shard_map/sub | solution.py:14
  229.6 3.6 while.11
  229.6 1.2 constant_dynamic-slice_fusion.3
  230.8 0.3 copy.15
  231.1 0.1 compare_convert_fusion.2
  231.2 2.1 fusion.12
  233.2 0.0 copy-start
  233.2 0.6 copy-done
  233.9 0.0 all-reduce.2.cloned.1.call-update
  233.9 170.1 %all-reduce.2.cloned.1.call-done = f32[128,128]{1,0:T(8,128)} async-done(((f32[128,128]{1,0:T(8,128)}), f32[128,128]{1,0:T(8,128)}) %all-reduce.2.cloned.1.call-update) | async-done | bytes 65552 | tf_op jit(solution)/shard_map/psum | solution.py:36
  404.0 1.3 constant_dynamic-slice_fusion.1
  (3 shorter events, 0.0 us)
Async XLA Ops:
  19.2 177.2 %all-to-all-start = ((f32[1536,12,128]{2,1,0:T(8,128)}), f32[1536,12,128]{2,1,0:T(8,128)}, u32[]{:S(2)}, u32[]{:S(2)}) async-start(f32[1536,12,128]{2,1,0:T(8,128)} %copy.7), calls=%async_computation | async-start | bytes 25165824 | tf_op jit(solution)/shard_map/all_to_all | solution.py:13
  31.1 372.9 %all-reduce.2.cloned.1.call-start = ((), (), s32[]{:S(2)}) async-start(), calls=%async_computation.1 | async-start | bytes 131072 | tf_op jit(solution)/shard_map/psum | solution.py:36
  233.2 0.6 copy-start
Sparse Core Ops, SparseCore 0:
  234.0 169.9 all-reduce.1
where the time goes:
time: 414 us; the launch traced here: 412 us
  waiting for transfers between devices  335 us (81%)
  local copies, waits for them, and re-layouts  38.3 us (9%)
  between operations  13.4 us (3%)
  starting transfers between devices  11.9 us (3%)
  other arithmetic  11 us (3%)
    psum x1, waiting for transfers between devices, body(): summed = lax.psum(partial_sum, ('row', 'col'))  170 us
    all_to_all x1, waiting for transfers between devices, body(): lax.all_to_all(cycle_inter, ('row', 'col'), split_axis=0, concat_axis=1,...  165 us
    all_to_all x2, local copies, waits for them, and re-layouts, body(): lax.all_to_all(cycle_inter, ('row', 'col'), split_axis=0, concat_axis=1,...  22.3 us
    unnamed x3, local copies, waits for them, and re-layouts  13.3 us
    all_to_all x1, starting transfers between devices, body(): lax.all_to_all(cycle_inter, ('row', 'col'), split_axis=0, concat_axis=1,...  11.9 us
    sub x1, other arithmetic, body(): amplitudes = cycle_inter - jnp.swapaxes(received, 0, 1)  10.9 us
  transfers between devices with their start and end apart: 2, of which 2 were waited for; matrix products, arithmetic and copies ran while one was open for 0% of the time, Pallas kernels for 0%

commit v1 on v0

--- a/solution.py
+++ b/solution.py
@@ -33,7 +33,7 @@
         0, needed_blocks, accumulate, jnp.zeros((occupied, slab_pairs), jnp.float32)
     )
     owned_rows = occupied // row_count
-    summed = lax.psum(partial_sum, ("row", "col"))
+    summed = lax.psum(lax.psum(partial_sum, "col"), "row")
     return lax.dynamic_slice_in_dim(summed, lax.axis_index("row") * owned_rows, owned_rows, 0)
 
 

time: 414 us -> 478 us (1.15)
  waiting for transfers between devices: 335 us -> 398 us
    psum x1 -> x2, waiting for transfers between devices: 170 us -> 233 us  [body(): summed = lax.psum(lax.psum(partial_sum, 'col'), 'row')]
  transfers between devices with their start and end apart: 2 -> 3, of which waited for: 2 -> 3; matrix products, arithmetic and copies ran while one was open for 0% -> 0% of each run, Pallas kernels for 0% -> 0%
where the time goes in v1:
time: 478 us; the launch traced here: 475 us
  waiting for transfers between devices  398 us (83%)
  local copies, waits for them, and re-layouts  38.3 us (8%)
  between operations  13.4 us (3%)
  starting transfers between devices  12 us (3%)
  other arithmetic  11 us (2%)
    psum x2, waiting for transfers between devices, body(): summed = lax.psum(lax.psum(partial_sum, 'col'), 'row')  233 us
    all_to_all x1, waiting for transfers between devices, body(): lax.all_to_all(cycle_inter, ('row', 'col'), split_axis=0, concat_axis=1,...  165 us
    all_to_all x2, local copies, waits for them, and re-layouts, body(): lax.all_to_all(cycle_inter, ('row', 'col'), split_axis=0, concat_axis=1,...  22.3 us
    unnamed x3, local copies, waits for them, and re-layouts  13.3 us
    all_to_all x1, starting transfers between devices, body(): lax.all_to_all(cycle_inter, ('row', 'col'), split_axis=0, concat_axis=1,...  11.9 us
    sub x1, other arithmetic, body(): amplitudes = cycle_inter - jnp.swapaxes(received, 0, 1)  10.9 us
  transfers between devices with their start and end apart: 3, of which 3 were waited for; matrix products, arithmetic and copies ran while one was open for 0% of the time, Pallas kernels for 0%

profile of v1, /device:TPU:1, one launch (start us, length us, event | category | flops | bytes accessed | tf_op | source)
XLA Modules:
  0.0 474.7 jit_solution(9486146143385767379)
XLA Ops:
  6.5 12.7 %copy.7 = f32[1536,12,128]{2,1,0:T(8,128)} copy(f32[1536,12,128]{2,0,1:T(8,128)} %param.4) | data formatting | bytes 18874368 | tf_op args[0]
  19.2 11.9 %all-to-all-start = ((f32[1536,12,128]{2,1,0:T(8,128)}), f32[1536,12,128]{2,1,0:T(8,128)}, u32[]{:S(2)}, u32[]{:S(2)}) async-start(f32[1536,12,128]{2,1,0:T(8,128)} %copy.7), calls=%async_computation | async-start | bytes 25165824 | tf_op jit(solution)/shard_map/all_to_all | solution.py:13
  31.1 0.0 all-reduce.3.cloned.1.call-start
  31.2 165.2 %all-to-all-done = f32[1536,12,128]{2,1,0:T(8,128)} async-done(((f32[1536,12,128]{2,1,0:T(8,128)}), f32[1536,12,128]{2,1,0:T(8,128)}, u32[]{:S(2)}, u32[]{:S(2)}) %all-to-all-start) | async-done | bytes 9437216 | tf_op jit(solution)/shard_map/all_to_all | solution.py:13
  196.3 10.3 %copy.9 = f32[12,128,12,128]{3,2,1,0:T(8,128)} copy(f32[12,128,12,128]{3,2,0,1:T(8,128)} %bitcast.2) | data formatting | bytes 18874368 | tf_op jit(solution)/shard_map/all_to_all | solution.py:13
  206.7 12.0 %all_to_all.16 = f32[12,1536,128]{2,1,0:T(8,128)} reshape(f32[12,128,12,128]{3,2,1,0:T(8,128)} %copy.9) | data formatting | bytes 18874368 | tf_op jit(solution)/shard_map/all_to_all | solution.py:13
  218.7 10.9 %bitcast_subtract_fusion = f32[1536,12,128]{2,0,1:T(8,128)} fusion(f32[1536,12,128]{2,0,1:T(8,128)} %param.4, f32[12,1536,128]{2,1,0:T(8,128)} %all_to_all.16), kind=kLoop, calls=%fused_computation.11 | loop fusion | flops 2359296 | bytes 28311552 | tf_op jit(solution)/shard_map/sub | solution.py:14
  229.6 3.6 while.11
  229.6 1.2 constant_dynamic-slice_fusion.3
  230.8 0.3 copy.15
  231.1 0.1 compare_convert_fusion.2
  231.2 2.1 fusion.12
  233.2 0.0 copy-start
  233.2 0.6 copy-done
  233.9 0.0 all-reduce.3.cloned.1.call-update
  233.9 0.0 all-reduce.5.cloned.1.call-start
  233.9 99.9 %all-reduce.3.cloned.1.call-done = f32[128,128]{1,0:T(8,128)} async-done(((f32[128,128]{1,0:T(8,128)}), f32[128,128]{1,0:T(8,128)}) %all-reduce.3.cloned.1.call-update) | async-done | bytes 65552 | tf_op jit(solution)/shard_map/psum | solution.py:36
  333.9 0.0 all-reduce.5.cloned.1.call-update
  333.9 132.7 %all-reduce.5.cloned.1.call-done = f32[128,128]{1,0:T(8,128)} async-done(((f32[128,128]{1,0:T(8,128)}), f32[128,128]{1,0:T(8,128)}) %all-reduce.5.cloned.1.call-update) | async-done | bytes 65552 | tf_op jit(solution)/shard_map/psum | solution.py:36
  466.6 1.3 constant_dynamic-slice_fusion.1
  (3 shorter events, 0.0 us)
Async XLA Ops:
  19.2 177.2 %all-to-all-start = ((f32[1536,12,128]{2,1,0:T(8,128)}), f32[1536,12,128]{2,1,0:T(8,128)}, u32[]{:S(2)}, u32[]{:S(2)}) async-start(f32[1536,12,128]{2,1,0:T(8,128)} %copy.7), calls=%async_computation | async-start | bytes 25165824 | tf_op jit(solution)/shard_map/all_to_all | solution.py:13
  31.1 302.8 %all-reduce.3.cloned.1.call-start = ((), (), s32[]{:S(2)}) async-start(), calls=%async_computation.1 | async-start | bytes 131072 | tf_op jit(solution)/shard_map/psum | solution.py:36
  233.2 0.6 copy-start
  233.9 232.7 %all-reduce.5.cloned.1.call-start = ((), (), s32[]{:S(2)}) async-start(), calls=%async_computation.2 | async-start | bytes 131072 | tf_op jit(solution)/shard_map/psum | solution.py:36
Sparse Core Ops, SparseCore 0:
  234.0 99.7 all-reduce.2
  336.5 130.0 all-reduce.4

commit v2 on v0

--- a/solution.py
+++ b/solution.py
@@ -33,7 +33,7 @@
         0, needed_blocks, accumulate, jnp.zeros((occupied, slab_pairs), jnp.float32)
     )
     owned_rows = occupied // row_count
-    summed = lax.psum(partial_sum, ("row", "col"))
+    summed = jnp.sum(lax.all_gather(partial_sum, ("row", "col")), axis=0)
     return lax.dynamic_slice_in_dim(summed, lax.axis_index("row") * owned_rows, owned_rows, 0)
 
 

time: 414 us -> 592 us (1.43)
  waiting for transfers between devices: 335 us -> 510 us
    all_gather x0 -> x1, waiting for transfers between devices: none -> 345 us  [body(): summed = jnp.sum(lax.all_gather(partial_sum, ('row', 'col')), axis=0)]
    psum x1 -> x0, waiting for transfers between devices: 170 us -> none  [body(): summed = lax.psum(partial_sum, ('row', 'col'))]
where the time goes in v2:
time: 592 us; the launch traced here: 590 us
  waiting for transfers between devices  510 us (86%)
  local copies, waits for them, and re-layouts  37.6 us (6%)
  other arithmetic  14.8 us (2%)
  between operations  13.4 us (2%)
  starting transfers between devices  11.9 us (2%)
    all_gather x1, waiting for transfers between devices, body(): summed = jnp.sum(lax.all_gather(partial_sum, ('row', 'col')), axis=0)  345 us
    all_to_all x1, waiting for transfers between devices, body(): lax.all_to_all(cycle_inter, ('row', 'col'), split_axis=0, concat_axis=1,...  165 us
    all_to_all x2, local copies, waits for them, and re-layouts, body(): lax.all_to_all(cycle_inter, ('row', 'col'), split_axis=0, concat_axis=1,...  22.3 us
    unnamed x3, local copies, waits for them, and re-layouts  13.3 us
    all_to_all x1, starting transfers between devices, body(): lax.all_to_all(cycle_inter, ('row', 'col'), split_axis=0, concat_axis=1,...  11.9 us
  transfers between devices with their start and end apart: 2, of which 2 were waited for; matrix products, arithmetic and copies ran while one was open for 0% of the time, Pallas kernels for 0%

profile of v2, /device:TPU:1, one launch (start us, length us, event | category | flops | bytes accessed | tf_op | source)
XLA Modules:
  0.0 590.2 jit_solution(13167373385702013728)
XLA Ops:
  6.5 12.7 %copy.7 = f32[1536,12,128]{2,1,0:T(8,128)} copy(f32[1536,12,128]{2,0,1:T(8,128)} %param.4) | data formatting | bytes 18874368 | tf_op args[0]
  19.2 11.9 %all-to-all-start = ((f32[1536,12,128]{2,1,0:T(8,128)}), f32[1536,12,128]{2,1,0:T(8,128)}, u32[]{:S(2)}, u32[]{:S(2)}) async-start(f32[1536,12,128]{2,1,0:T(8,128)} %copy.7), calls=%async_computation | async-start | bytes 25165824 | tf_op jit(solution)/shard_map/all_to_all | solution.py:13
  31.1 0.0 all-gather.3.cloned.1.call-start
  31.2 165.2 %all-to-all-done = f32[1536,12,128]{2,1,0:T(8,128)} async-done(((f32[1536,12,128]{2,1,0:T(8,128)}), f32[1536,12,128]{2,1,0:T(8,128)}, u32[]{:S(2)}, u32[]{:S(2)}) %all-to-all-start) | async-done | bytes 9437216 | tf_op jit(solution)/shard_map/all_to_all | solution.py:13
  196.3 10.3 %copy.9 = f32[12,128,12,128]{3,2,1,0:T(8,128)} copy(f32[12,128,12,128]{3,2,0,1:T(8,128)} %bitcast.2) | data formatting | bytes 18874368 | tf_op jit(solution)/shard_map/all_to_all | solution.py:13
  206.7 12.0 %all_to_all.16 = f32[12,1536,128]{2,1,0:T(8,128)} reshape(f32[12,128,12,128]{3,2,1,0:T(8,128)} %copy.9) | data formatting | bytes 18874368 | tf_op jit(solution)/shard_map/all_to_all | solution.py:13
  218.7 10.9 %bitcast_subtract_fusion = f32[1536,12,128]{2,0,1:T(8,128)} fusion(f32[1536,12,128]{2,0,1:T(8,128)} %param.4, f32[12,1536,128]{2,1,0:T(8,128)} %all_to_all.16), kind=kLoop, calls=%fused_computation.11 | loop fusion | flops 2359296 | bytes 28311552 | tf_op jit(solution)/shard_map/sub | solution.py:14
  229.6 3.6 while.11
  229.6 1.2 constant_dynamic-slice_fusion.3
  230.8 0.3 copy.15
  231.1 0.1 compare_convert_fusion.2
  231.2 2.1 fusion.12
  233.2 0.0 copy-start
  233.2 0.6 copy-done
  233.9 0.0 all-gather.3.cloned.1.call-update
  233.9 345.1 %all-gather.3.cloned.1.call-done = f32[16384,128]{1,0:T(8,128)} async-done(((f32[128,128]{1,0:T(8,128)}), f32[16384,128]{1,0:T(8,128)}) %all-gather.3.cloned.1.call-update) | async-done | bytes 8388624 | tf_op jit(solution)/shard_map/all_gather | solution.py:36
  579.0 3.8 reduce_sum.9
  582.8 0.6 constant_dynamic-slice_fusion.1
  (3 shorter events, 0.0 us)
Async XLA Ops:
  19.2 177.2 %all-to-all-start = ((f32[1536,12,128]{2,1,0:T(8,128)}), f32[1536,12,128]{2,1,0:T(8,128)}, u32[]{:S(2)}, u32[]{:S(2)}) async-start(f32[1536,12,128]{2,1,0:T(8,128)} %copy.7), calls=%async_computation | async-start | bytes 25165824 | tf_op jit(solution)/shard_map/all_to_all | solution.py:13
  31.1 547.9 %all-gather.3.cloned.1.call-start = ((), (), s32[]{:S(2)}) async-start(), calls=%async_computation.1 | async-start | bytes 8454144 | tf_op jit(solution)/shard_map/all_gather | solution.py:36
  233.2 0.6 copy-start
Sparse Core Ops, SparseCore 0:
  234.0 344.9 all-gather.2
